TPU v7x, 512 devices: a whole 4x8x8 slice. The times are simulated.
512 devices in a mesh: dp: 32 (over z, x), tensor: 16 (over y, core).
Axes of the slice: x: 4, y: 8, z: 8, core: 2. Of those that a mesh axis runs over, the one named last changes fastest.
Arguments:
- tokens: bfloat16 [16384, 8192], P('dp', 'tensor'), may hold values from -6 to 6
- key_value_weight: bfloat16 [8192, 2048], P('tensor'), may hold values from -0.0625 to 0.0625
- adapter_down_weight: bfloat16 [96, 64, 8192], P('dp', None, 'tensor'), may hold values from -0.0625 to 0.0625
- adapter_up_weight: bfloat16 [96, 64, 2048], P('dp', None, 'tensor'), may hold values from -0.75 to 0.75
- cotangent: bfloat16 [16384, 2048], P('dp', 'tensor'), may hold values from -3 to 3
- sequence_adapter_index: int32 [512], replicated, may hold values from 0 to 95, as said below
- adapter_storage_row: int32 [96], replicated, may hold values from 0 to 95, as said below
Outputs:
- key_value_output: bfloat16 [16384, 2048], P('dp', 'tensor')
- token_gradient: bfloat16 [16384, 8192], P('dp', 'tensor')
- grad_down: float32 [96, 64, 8192], P('dp', None, 'tensor')
- grad_up: float32 [96, 64, 2048], P('dp', None, 'tensor')
Inputs may be any that keep to these rules, and one draw needn't show every extreme that they name: Each value appears once: adapter a is held at row adapter_storage_row[a] of adapter_down_weight, adapter_up_weight, grad_down and grad_up, on index adapter_storage_row[a] // 3 of dp. `sequence_adapter_index`: the 16 sequences i that share one value of i // 16 use adapters held on 16 different indices of dp.
All inputs are finite; a program needn't handle non-finite values.
Results may differ from a plain program's by a relative error of at most 0.02.
Values may be sent and summed in bfloat16 or wider, within the bound.
No kernel may reach another device: no remote copies, remote signals or barrier semaphores. Data moves between devices by JAX's collectives and lax.ppermute only.
A program may use at most 64 MiB of HBM per device.

v0:
```python
import jax
import jax.numpy as jnp
from jax import lax
from jax.sharding import PartitionSpec as P

adapter_scale = 0.25


def gathered_total(value, axis):
    return lax.all_gather(value, axis).astype(jnp.float32).sum(0)


def cut_along(value, dim, length):
    before, after = (value.shape[:dim], value.shape[dim + 1 :])
    return jnp.moveaxis(value.reshape(*before, length, -1, *after), dim, 0)


def sent_and_summed(value, axis, dim):
    pieces = cut_along(value, dim, lax.axis_size(axis))
    arrived = lax.all_to_all(pieces, axis, split_axis=0, concat_axis=0, tiled=True)
    return arrived.astype(jnp.float32).sum(axis=0)


def on_device(
    tokens,
    key_value_weight,
    adapter_down_weight,
    adapter_up_weight,
    cotangent,
    sequence_adapter_index,
    adapter_storage_row,
):
    dp_count = lax.axis_size("dp")
    my_index = lax.axis_index("dp")
    resident_adapters = adapter_down_weight.shape[0]
    rank_span = adapter_down_weight.shape[1]
    block_span = adapter_down_weight.shape[2]
    output_block = adapter_up_weight.shape[2]
    token_row_matrix = tokens.shape[0]
    adapters = adapter_storage_row.shape[0]
    seq_local = sequence_adapter_index.shape[0] // dp_count
    seq_length = token_row_matrix // seq_local
    adapter_codes = jnp.arange(adapters, dtype=jnp.int32)
    matches = sequence_adapter_index[:, None] == adapter_codes[None, :]
    seq_rows = jnp.sum(jnp.where(matches, adapter_storage_row[None, :], 0), axis=1)
    my_rows = lax.dynamic_slice_in_dim(seq_rows, my_index * seq_local, seq_local)
    my_owners = my_rows // resident_adapters
    owner_codes = jnp.arange(dp_count, dtype=jnp.int32)
    from_owner = (my_owners[:, None] == owner_codes[None, :]).astype(jnp.bfloat16)
    reader_rows = seq_rows.reshape(dp_count, seq_local)
    local_codes = jnp.arange(resident_adapters, dtype=jnp.int32) + my_index * resident_adapters
    wanted = (reader_rows[:, :, None] == local_codes[None, None, :]).astype(jnp.float32)
    serve_table = jnp.sum(wanted, axis=1).astype(jnp.bfloat16)
    usage_count = jnp.sum(wanted, axis=(0, 1))
    inverse_use = 1.0 / jnp.maximum(usage_count, 1.0)
    down_flattened = adapter_down_weight.reshape(resident_adapters, rank_span * block_span)
    up_flattened = adapter_up_weight.reshape(resident_adapters, rank_span * output_block)
    send_down = jnp.dot(serve_table, down_flattened, preferred_element_type=jnp.float32).astype(
        jnp.bfloat16
    )
    send_up = jnp.dot(serve_table, up_flattened, preferred_element_type=jnp.float32).astype(
        jnp.bfloat16
    )
    came_down, came_up = (
        lax.all_to_all(send_down, "dp", split_axis=0, concat_axis=0, tiled=True),
        lax.all_to_all(send_up, "dp", split_axis=0, concat_axis=0, tiled=True),
    )
    got_down = jnp.dot(from_owner, came_down, preferred_element_type=jnp.float32)
    got_up = jnp.dot(from_owner, came_up, preferred_element_type=jnp.float32)
    storage_down = got_down.astype(jnp.bfloat16).reshape(seq_local, rank_span, block_span)
    storage_up = got_up.astype(jnp.bfloat16).reshape(seq_local, rank_span, output_block)
    token_sequences = tokens.reshape(seq_local, seq_length, block_span)
    cot_seqs = cotangent.reshape(seq_local, seq_length, output_block)
    inner_part = jnp.einsum(
        "jby,jcy->jbc", token_sequences, storage_down, preferred_element_type=jnp.float32
    )
    back_part = jnp.einsum("slo,sro->slr", cot_seqs, storage_up, preferred_element_type=jnp.float32)
    joined = gathered_total(
        jnp.concatenate([inner_part, back_part], axis=2).astype(jnp.bfloat16), "tensor"
    ).astype(jnp.float32)
    middle_round = joined[:, :, :rank_span].astype(jnp.bfloat16)
    backward_round = joined[:, :, rank_span:].astype(jnp.bfloat16)
    partial_value = jnp.dot(tokens, key_value_weight, preferred_element_type=jnp.float32)
    frozen_backbone = sent_and_summed(partial_value.astype(jnp.bfloat16), "tensor", 1)
    adapter_output = jnp.einsum(
        "ivq,iqg->ivg", middle_round, storage_up, preferred_element_type=jnp.float32
    )
    key_value_output = (
        frozen_backbone + adapter_scale * adapter_output.reshape(token_row_matrix, output_block)
    ).astype(jnp.bfloat16)
    base_gradient = lax.dot_general(
        lax.all_gather(cotangent, "tensor", axis=1, tiled=True),
        key_value_weight,
        (((1,), (1,)), ((), ())),
        preferred_element_type=jnp.float32,
    )
    adapter_gradient = jnp.einsum(
        "cun,cny->cuy", backward_round, storage_down, preferred_element_type=jnp.float32
    )
    token_gradient = (
        base_gradient + adapter_scale * adapter_gradient.reshape(token_row_matrix, block_span)
    ).astype(jnp.bfloat16)
    down_term = (
        adapter_scale
        * jnp.einsum(
            "cfj,cfh->cjh", backward_round, token_sequences, preferred_element_type=jnp.float32
        )
    ).astype(jnp.bfloat16)
    up_term = (
        adapter_scale
        * jnp.einsum("slr,slo->sro", middle_round, cot_seqs, preferred_element_type=jnp.float32)
    ).astype(jnp.bfloat16)
    to_owner = from_owner.T
    ship_down = jnp.dot(
        to_owner, down_term.reshape(seq_local, -1), preferred_element_type=jnp.float32
    ).astype(jnp.bfloat16)
    ship_up = jnp.dot(
        to_owner, up_term.reshape(seq_local, -1), preferred_element_type=jnp.float32
    ).astype(jnp.bfloat16)
    back_down, back_up = (
        lax.all_to_all(ship_down, "dp", split_axis=0, concat_axis=0, tiled=True),
        lax.all_to_all(ship_up, "dp", split_axis=0, concat_axis=0, tiled=True),
    )
    serve_turned = serve_table.T
    grad_down = (
        jnp.dot(serve_turned, back_down, preferred_element_type=jnp.float32) * inverse_use[:, None]
    )
    grad_up = (
        jnp.dot(serve_turned, back_up, preferred_element_type=jnp.float32) * inverse_use[:, None]
    )
    grad_down = grad_down.reshape(resident_adapters, rank_span, block_span)
    grad_up = grad_up.reshape(resident_adapters, rank_span, output_block)
    return (key_value_output, token_gradient, grad_down, grad_up)


def solution(mesh):
    in_specs = (
        P("dp", "tensor"),
        P("tensor", None),
        P("dp", None, "tensor"),
        P("dp", None, "tensor"),
        P("dp", "tensor"),
        P(),
        P(),
    )
    out_specs = (
        P("dp", "tensor"),
        P("dp", "tensor"),
        P("dp", None, "tensor"),
        P("dp", None, "tensor"),
    )
    return jax.shard_map(
        on_device, mesh=mesh, in_specs=in_specs, out_specs=out_specs, check_vma=False
    )
```

profile of v0, /device:TPU:24, one launch (start us, length us, event | category | flops | bytes accessed | tf_op | source)
XLA Modules:
  0.0 297.3 jit_solution(2475872210258353637)
XLA Ops:
  12.4 13.2 %all-to-all-start.2 = ((bf16[32,2,4096]{2,1,0:T(2,128)(2,1)}), bf16[32,2,4096]{2,1,0:T(2,128)(2,1)S(1)}, u32[]{:S(2)}, u32[]{:S(2)}) async-start(bf16[32,2,4096]{2,1,0:T(2,128)(2,1)} %reshape.109), calls=%async_computation.2 | async-start | bytes 1048576 | tf_op jit(solution)/shard_map/all_to_all | solution.py:66
  25.7 2.1 fusion
  27.8 4.6 %reduce.2 = bf16[32,32768]{1,0:T(8,128)(2,1)} reduce(bf16[32,1,32768]{2,0,1:T(8,128)(2,1)} %fusion, bf16[]{:T(256)} %broadcast.29), dimensions={1}, to_apply=%copy.23.reduce_sub_computation | reduce | bytes 4194306 | tf_op jit(solution)/shard_map/all_to_all | solution.py:65
  32.4 4.5 %reshape.111 = bf16[32,2,16384]{2,1,0:T(2,128)(2,1)} reshape(bf16[32,32768]{1,0:T(8,128)(2,1)} %reduce.2) | data formatting | bytes 4194304
  36.9 6.4 %all-to-all-done.2 = bf16[32,2,4096]{2,1,0:T(2,128)(2,1)S(1)} async-done(((bf16[32,2,4096]{2,1,0:T(2,128)(2,1)}), bf16[32,2,4096]{2,1,0:T(2,128)(2,1)S(1)}, u32[]{:S(2)}, u32[]{:S(2)}) %all-to-all-start.2) | async-done | bytes 524320 | tf_op jit(solution)/shard_map/all_to_all | solution.py:66
  43.3 4.8 %all-to-all-start.1 = ((bf16[32,2,16384]{2,1,0:T(2,128)(2,1)}), bf16[32,2,16384]{2,1,0:T(2,128)(2,1)}, u32[]{:S(2)}, u32[]{:S(2)}) async-start(bf16[32,2,16384]{2,1,0:T(2,128)(2,1)} %reshape.111), calls=%async_computation.1 | async-start | bytes 4194304 | tf_op jit(solution)/shard_map/all_to_all | solution.py:65
  48.2 3.6 %reshape.110 = bf16[32,1,8192]{2,1,0:T(2,128)(2,1)S(1)} reshape(bf16[32,2,4096]{2,1,0:T(2,128)(2,1)} %copy-done.1) | data formatting | bytes 1048576
  53.5 43.8 %all-to-all-done.1 = bf16[32,2,16384]{2,1,0:T(2,128)(2,1)} async-done(((bf16[32,2,16384]{2,1,0:T(2,128)(2,1)}), bf16[32,2,16384]{2,1,0:T(2,128)(2,1)}, u32[]{:S(2)}, u32[]{:S(2)}) %all-to-all-start.1) | async-done | bytes 2097184 | tf_op jit(solution)/shard_map/all_to_all | solution.py:65
  97.3 10.5 %reshape.112 = bf16[32,1,32768]{2,1,0:T(2,128)(2,1)} reshape(bf16[32,2,16384]{2,1,0:T(2,128)(2,1)} %all-to-all-done.1) | data formatting | bytes 4194304
  107.8 4.6 %convolution_convert_fusion.2 = bf16[16,32768]{1,0:T(8,128)(2,1)S(1)} fusion(bf16[32,1,32768]{2,1,0:T(2,128)(2,1)} %reshape.112, s32[16]{0:T(128)S(1)} %and_select_fusion), kind=kOutput, calls=%fused_computation.4 | convolution fusion | flops 34079232 | bytes 3145792 | tf_op jit(solution)/shard_map/dot_general | solution.py:68
  114.0 2.3 fusion.8
  116.3 1.8 copy.67
  118.2 7.3 %all-to-all-start = ((bf16[16,512,128]{2,1,0:T(8,128)(2,1)}), bf16[16,512,128]{2,1,0:T(8,128)(2,1)}, u32[]{:S(2)}, u32[]{:S(2)}) async-start(bf16[16,512,128]{2,1,0:T(8,128)(2,1)} %bitcast.89), calls=%async_computation | async-start | bytes 4194304 | tf_op jit(solution)/shard_map/all_to_all | solution.py:20
  125.5 54.0 %all-gather.3.cloned.1.call-done = bf16[16,16,32,128]{3,2,1,0:T(8,128)(2,1)} async-done(((bf16[1,16,32,128]{3,2,1,0:T(8,128)(2,1)}), bf16[16,16,32,128]{3,2,1,0:T(8,128)(2,1)}) %all-gather.3.cloned.1.call-update) | async-done | bytes 2097168 | tf_op jit(solution)/shard_map/all_gather | solution.py:10
  179.5 1.9 reduce
  183.8 2.7 reduce.4
  186.5 2.2 reshape.115
  188.8 11.6 %all-to-all-start.4 = ((bf16[32,2,4096]{2,1,0:T(2,128)(2,1)}), bf16[32,2,4096]{2,1,0:T(2,128)(2,1)}, u32[]{:S(2)}, u32[]{:S(2)}) async-start(bf16[32,2,4096]{2,1,0:T(2,128)(2,1)} %reshape.115), calls=%async_computation.4 | async-start | bytes 1048576 | tf_op jit(solution)/shard_map/all_to_all | solution.py:122
  201.1 1.9 multiply_convert_fusion
  203.6 2.2 fusion.1
  205.7 4.5 %reduce.3 = bf16[32,32768]{1,0:T(8,128)(2,1)} reduce(bf16[32,1,32768]{2,0,1:T(8,128)(2,1)} %fusion.1, bf16[]{:T(256)} %broadcast.29), dimensions={1}, to_apply=%copy.25.reduce_sub_computation | reduce | bytes 4194306 | tf_op jit(solution)/shard_map/all_to_all | solution.py:121
  210.3 4.5 %reshape.113 = bf16[32,2,16384]{2,1,0:T(2,128)(2,1)} reshape(bf16[32,32768]{1,0:T(8,128)(2,1)} %reduce.3) | data formatting | bytes 4194304
  214.8 3.8 %all-to-all-done.4 = bf16[32,2,4096]{2,1,0:T(2,128)(2,1)} async-done(((bf16[32,2,4096]{2,1,0:T(2,128)(2,1)}), bf16[32,2,4096]{2,1,0:T(2,128)(2,1)}, u32[]{:S(2)}, u32[]{:S(2)}) %all-to-all-start.4) | async-done | bytes 524320 | tf_op jit(solution)/shard_map/all_to_all | solution.py:122
  218.6 6.0 %all-to-all-start.3 = ((bf16[32,2,16384]{2,1,0:T(2,128)(2,1)}), bf16[32,2,16384]{2,1,0:T(2,128)(2,1)}, u32[]{:S(2)}, u32[]{:S(2)}) async-start(bf16[32,2,16384]{2,1,0:T(2,128)(2,1)} %reshape.113), calls=%async_computation.3 | async-start | bytes 4194304 | tf_op jit(solution)/shard_map/all_to_all | solution.py:121
  224.6 1.9 convert_reduce_fusion
  227.5 1.3 convolution_multiply_fusion.2
  228.8 16.4 %all-gather.5.cloned.1.call-done = bf16[512,2048]{1,0:T(8,128)(2,1)} async-done(((bf16[512,128]{1,0:T(8,128)(2,1)}), bf16[512,2048]{1,0:T(8,128)(2,1)}) %all-gather.5.cloned.1.call-update) | async-done | bytes 2097168 | tf_op jit(solution)/shard_map/all_gather | solution.py:92
  245.2 3.9 %fusion.9 = bf16[512,512]{1,0:T(8,128)(2,1)} fusion(f32[512,512]{1,0:T(8,128)} %bitcast.101, bf16[512,2048]{1,0:T(8,128)(2,1)} %all-gather.5.cloned.1.call-done, bf16[512,2048]{1,0:T(8,128)(2,1)S(1)} %copy-done), kind=kOutput, calls=%fused_computation.23 | convolution fusion | flops 1074266112 | bytes 5767168 | tf_op jit(solution)/shard_map/dot_general | solution.py:91
  249.1 3.6 %reshape.116 = bf16[32,1,8192]{2,1,0:T(2,128)(2,1)S(1)} reshape(bf16[32,2,4096]{2,1,0:T(2,128)(2,1)} %all-to-all-done.4) | data formatting | bytes 1048576
  254.1 20.5 %all-to-all-done.3 = bf16[32,2,16384]{2,1,0:T(2,128)(2,1)} async-done(((bf16[32,2,16384]{2,1,0:T(2,128)(2,1)}), bf16[32,2,16384]{2,1,0:T(2,128)(2,1)}, u32[]{:S(2)}, u32[]{:S(2)}) %all-to-all-start.3) | async-done | bytes 2097184 | tf_op jit(solution)/shard_map/all_to_all | solution.py:121
  274.6 10.5 %reshape.114 = bf16[32,1,32768]{2,1,0:T(2,128)(2,1)} reshape(bf16[32,2,16384]{2,1,0:T(2,128)(2,1)} %all-to-all-done.3) | data formatting | bytes 4194304
  285.0 4.5 %convolution_multiply_fusion = f32[3,32768]{1,0:T(4,128)S(1)} fusion(bf16[32,3]{0,1:T(4,128)(2,1)S(1)} %get-tuple-element.5, bf16[32,1,32768]{2,1,0:T(2,128)(2,1)} %reshape.114, f32[3]{0:T(128)S(1)} %maximum_divide_fusion), kind=kOutput, calls=%fused_computation.5 | convolution fusion | flops 6389760 | bytes 2490572 | tf_op jit(solution)/shard_map/dot_general | solution.py:126
  (43 shorter events, 15.6 us)
Async XLA Ops:
  7.2 106.9 %copy-start = (bf16[512,2048]{1,0:T(8,128)(2,1)S(1)}, bf16[512,2048]{1,0:T(8,128)(2,1)}, u32[]{:S(2)}) copy-start(bf16[512,2048]{1,0:T(8,128)(2,1)} %param.8) | copy-start | bytes 6291460
  7.2 18.4 %copy-start.5 = (bf16[3,64,512]{2,1,0:T(8,128)(2,1)S(1)}, bf16[3,64,512]{2,1,0:T(8,128)(2,1)}, u32[]{:S(2)}) copy-start(bf16[3,64,512]{2,1,0:T(8,128)(2,1)} %param.9) | copy-start | bytes 589828
  12.4 30.9 %all-to-all-start.2 = ((bf16[32,2,4096]{2,1,0:T(2,128)(2,1)}), bf16[32,2,4096]{2,1,0:T(2,128)(2,1)S(1)}, u32[]{:S(2)}, u32[]{:S(2)}) async-start(bf16[32,2,4096]{2,1,0:T(2,128)(2,1)} %reshape.109), calls=%async_computation.2 | async-start | bytes 1048576 | tf_op jit(solution)/shard_map/all_to_all | solution.py:66
  43.3 4.9 %copy-start.1 = (bf16[32,2,4096]{2,1,0:T(2,128)(2,1)}, bf16[32,2,4096]{2,1,0:T(2,128)(2,1)S(1)}, u32[]{:S(2)}) copy-start(bf16[32,2,4096]{2,1,0:T(2,128)(2,1)S(1)} %all-to-all-done.2) | copy-start | bytes 1572868
  43.3 54.0 %all-to-all-start.1 = ((bf16[32,2,16384]{2,1,0:T(2,128)(2,1)}), bf16[32,2,16384]{2,1,0:T(2,128)(2,1)}, u32[]{:S(2)}, u32[]{:S(2)}) async-start(bf16[32,2,16384]{2,1,0:T(2,128)(2,1)} %reshape.111), calls=%async_computation.1 | async-start | bytes 4194304 | tf_op jit(solution)/shard_map/all_to_all | solution.py:65
  48.1 4.5 %copy-start.3 = (bf16[512,128]{1,0:T(8,128)(2,1)S(1)}, bf16[512,128]{1,0:T(8,128)(2,1)}, u32[]{:S(2)}) copy-start(bf16[512,128]{1,0:T(8,128)(2,1)} %param.11) | copy-start | bytes 393220
  48.1 131.4 %all-gather.3.cloned.1.call-start = ((), (), s32[]{:S(2)}) async-start(), calls=%async_computation.5 | async-start | bytes 2228224 | tf_op jit(solution)/shard_map/all_gather | solution.py:10
  107.8 4.9 %copy-start.2 = (bf16[512,512]{1,0:T(8,128)(2,1)S(1)}, bf16[512,512]{1,0:T(8,128)(2,1)}, u32[]{:S(2)}) copy-start(bf16[512,512]{1,0:T(8,128)(2,1)} %param.7) | copy-start | bytes 1572868
  112.3 0.9 copy-start.4
  118.2 70.6 %all-to-all-start = ((bf16[16,512,128]{2,1,0:T(8,128)(2,1)}), bf16[16,512,128]{2,1,0:T(8,128)(2,1)}, u32[]{:S(2)}, u32[]{:S(2)}) async-start(bf16[16,512,128]{2,1,0:T(8,128)(2,1)} %bitcast.89), calls=%async_computation | async-start | bytes 4194304 | tf_op jit(solution)/shard_map/all_to_all | solution.py:20
  188.8 29.8 %all-to-all-start.4 = ((bf16[32,2,4096]{2,1,0:T(2,128)(2,1)}), bf16[32,2,4096]{2,1,0:T(2,128)(2,1)}, u32[]{:S(2)}, u32[]{:S(2)}) async-start(bf16[32,2,4096]{2,1,0:T(2,128)(2,1)} %reshape.115), calls=%async_computation.4 | async-start | bytes 1048576 | tf_op jit(solution)/shard_map/all_to_all | solution.py:122
  200.4 44.8 %all-gather.5.cloned.1.call-start = ((), (), s32[]{:S(2)}) async-start(), calls=%async_computation.6 | async-start | bytes 2228224 | tf_op jit(solution)/shard_map/all_gather | solution.py:92
  218.6 56.0 %all-to-all-start.3 = ((bf16[32,2,16384]{2,1,0:T(2,128)(2,1)}), bf16[32,2,16384]{2,1,0:T(2,128)(2,1)}, u32[]{:S(2)}, u32[]{:S(2)}) async-start(bf16[32,2,16384]{2,1,0:T(2,128)(2,1)} %reshape.113), calls=%async_computation.3 | async-start | bytes 4194304 | tf_op jit(solution)/shard_map/all_to_all | solution.py:121
Sparse Core Ops, SparseCore 0:
  114.2 65.3 all-gather.2
  203.3 41.8 all-gather.4
where the time goes:
time: 299 us; the launch traced here: 297 us
  waiting for transfers between devices  146 us (49%)
  local copies, waits for them, and re-layouts  45.9 us (15%)
  starting transfers between devices  43 us (14%)
  matrix products  29.1 us (10%)
  other arithmetic  19.4 us (6%)
  between operations  14.2 us (5%)
    all_gather x1, waiting for transfers between devices, gathered_total(): return lax.all_gather(value, axis).astype(jnp.float32).sum(0)  54 us
    all_to_all x1, waiting for transfers between devices, on_device(): lax.all_to_all(send_down, 'dp', split_axis=0, concat_axis=0, tiled=True)  43.8 us
    unnamed x26, local copies, waits for them, and re-layouts  43.4 us
    all_to_all x1, waiting for transfers between devices, on_device(): lax.all_to_all(ship_down, 'dp', split_axis=0, concat_axis=0, tiled=True)  20.5 us
    all_gather x1, waiting for transfers between devices, on_device(): lax.all_gather(cotangent, 'tensor', axis=1, tiled=True)  16.4 us
    all_to_all x1, starting transfers between devices, on_device(): lax.all_to_all(send_up, 'dp', split_axis=0, concat_axis=0, tiled=True)  13.2 us
    all_to_all x1, starting transfers between devices, on_device(): lax.all_to_all(ship_up, 'dp', split_axis=0, concat_axis=0, tiled=True)  11.6 us
    all_to_all x1, starting transfers between devices, sent_and_summed(): lax.all_to_all(pieces, axis, split_axis=0, concat_axis=0, tiled=True)  7.34 us
  transfers between devices with their start and end apart: 7, of which 6 were waited for; matrix products, arithmetic and copies ran while one was open for 19% of the time, Pallas kernels for 0%

commit v1 on v0

--- a/solution.py
+++ b/solution.py
@@ -4,6 +4,13 @@
 from jax.sharding import PartitionSpec as P
 
 adapter_scale = 0.25
+
+
+def all_by_exchange(x, axis, dim):
+    n_dev = lax.axis_size(axis)
+    parts = jnp.stack([x for _ in range(n_dev)])
+    parts = lax.all_to_all(parts, axis, split_axis=0, concat_axis=0)
+    return jnp.concatenate(parts, axis=dim)
 
 
 def gathered_total(value, axis):
@@ -89,7 +96,7 @@
         frozen_backbone + adapter_scale * adapter_output.reshape(token_row_matrix, output_block)
     ).astype(jnp.bfloat16)
     base_gradient = lax.dot_general(
-        lax.all_gather(cotangent, "tensor", axis=1, tiled=True),
+        all_by_exchange(cotangent, "tensor", 1),
         key_value_weight,
         (((1,), (1,)), ((), ())),
         preferred_element_type=jnp.float32,

time: 299 us -> 319 us (1.067)
  the two profiles are of different devices: /device:TPU:24 before, /device:TPU:4 now
where the time goes in v1:
time: 319 us; the launch traced here: 317 us
  waiting for transfers between devices  165 us (52%)
  local copies, waits for them, and re-layouts  49.1 us (15%)
  starting transfers between devices  42.7 us (13%)
  matrix products  26.8 us (8%)
  other arithmetic  19.3 us (6%)
  between operations  14.3 us (4%)
    all_to_all x1, waiting for transfers between devices, on_device(): lax.all_to_all(send_down, 'dp', split_axis=0, concat_axis=0, tiled=True)  46.5 us
    unnamed x29, local copies, waits for them, and re-layouts  44.2 us
    all_to_all x1, waiting for transfers between devices, on_device(): lax.all_to_all(ship_down, 'dp', split_axis=0, concat_axis=0, tiled=True)  37.6 us
    all_to_all x1, waiting for transfers between devices, sent_and_summed(): lax.all_to_all(pieces, axis, split_axis=0, concat_axis=0, tiled=True)  31.3 us
    all_to_all x1, waiting for transfers between devices, all_by_exchange(): parts = lax.all_to_all(parts, axis, split_axis=0, concat_axis=0)  27.9 us
    all_to_all x1, starting transfers between devices, on_device(): lax.all_to_all(send_up, 'dp', split_axis=0, concat_axis=0, tiled=True)  13.4 us
    all_gather x1, waiting for transfers between devices, gathered_total(): return lax.all_gather(value, axis).astype(jnp.float32).sum(0)  12.8 us
    all_to_all x1, starting transfers between devices, sent_and_summed(): lax.all_to_all(pieces, axis, split_axis=0, concat_axis=0, tiled=True)  7.26 us
  transfers between devices with their start and end apart: 7, of which 7 were waited for; matrix products, arithmetic and copies ran while one was open for 23% of the time, Pallas kernels for 0%

profile of v1, /device:TPU:4, one launch (start us, length us, event | category | flops | bytes accessed | tf_op | source)
XLA Modules:
  0.0 317.1 jit_solution(8084375405574795370)
XLA Ops:
  12.4 13.4 %all-to-all-start.2 = ((bf16[32,2,4096]{2,1,0:T(2,128)(2,1)}), bf16[32,2,4096]{2,1,0:T(2,128)(2,1)S(1)}, u32[]{:S(2)}, u32[]{:S(2)}) async-start(bf16[32,2,4096]{2,1,0:T(2,128)(2,1)} %reshape.119), calls=%async_computation.2 | async-start | bytes 1048576 | tf_op jit(solution)/shard_map/all_to_all | solution.py:73
  26.0 2.1 fusion
  28.1 4.5 %reduce.2 = bf16[32,32768]{1,0:T(8,128)(2,1)} reduce(bf16[32,1,32768]{2,0,1:T(8,128)(2,1)} %fusion, bf16[]{:T(256)} %broadcast.31), dimensions={1}, to_apply=%copy.26.reduce_sub_computation | reduce | bytes 4194306 | tf_op jit(solution)/shard_map/all_to_all | solution.py:72
  32.6 4.5 %reshape.121 = bf16[32,2,16384]{2,1,0:T(2,128)(2,1)} reshape(bf16[32,32768]{1,0:T(8,128)(2,1)} %reduce.2) | data formatting | bytes 4194304
  37.1 5.5 %all-to-all-done.2 = bf16[32,2,4096]{2,1,0:T(2,128)(2,1)S(1)} async-done(((bf16[32,2,4096]{2,1,0:T(2,128)(2,1)}), bf16[32,2,4096]{2,1,0:T(2,128)(2,1)S(1)}, u32[]{:S(2)}, u32[]{:S(2)}) %all-to-all-start.2) | async-done | bytes 524320 | tf_op jit(solution)/shard_map/all_to_all | solution.py:73
  42.6 5.6 %all-to-all-start.1 = ((bf16[32,2,16384]{2,1,0:T(2,128)(2,1)}), bf16[32,2,16384]{2,1,0:T(2,128)(2,1)}, u32[]{:S(2)}, u32[]{:S(2)}) async-start(bf16[32,2,16384]{2,1,0:T(2,128)(2,1)} %reshape.121), calls=%async_computation.1 | async-start | bytes 4194304 | tf_op jit(solution)/shard_map/all_to_all | solution.py:72
  49.6 1.9 copy.71
  51.5 46.5 %all-to-all-done.1 = bf16[32,2,16384]{2,1,0:T(2,128)(2,1)} async-done(((bf16[32,2,16384]{2,1,0:T(2,128)(2,1)}), bf16[32,2,16384]{2,1,0:T(2,128)(2,1)}, u32[]{:S(2)}, u32[]{:S(2)}) %all-to-all-start.1) | async-done | bytes 2097184 | tf_op jit(solution)/shard_map/all_to_all | solution.py:72
  98.0 7.3 %all-to-all-start = ((bf16[16,512,128]{2,1,0:T(8,128)(2,1)}), bf16[16,512,128]{2,1,0:T(8,128)(2,1)}, u32[]{:S(2)}, u32[]{:S(2)}) async-start(bf16[16,512,128]{2,1,0:T(8,128)(2,1)} %bitcast.92), calls=%async_computation | async-start | bytes 4194304 | tf_op jit(solution)/shard_map/all_to_all | solution.py:27
  105.4 3.6 %reshape.120 = bf16[32,1,8192]{2,1,0:T(2,128)(2,1)S(1)} reshape(bf16[32,2,4096]{2,1,0:T(2,128)(2,1)} %copy-done.1) | data formatting | bytes 1048576
  110.6 10.5 %reshape.122 = bf16[32,1,32768]{2,1,0:T(2,128)(2,1)} reshape(bf16[32,2,16384]{2,1,0:T(2,128)(2,1)} %all-to-all-done.1) | data formatting | bytes 4194304
  121.1 4.6 %convolution_convert_fusion.2 = bf16[16,32768]{1,0:T(8,128)(2,1)S(1)} fusion(bf16[32,1,32768]{2,1,0:T(2,128)(2,1)} %reshape.122, s32[16]{0:T(128)S(1)} %and_select_fusion), kind=kOutput, calls=%fused_computation.4 | convolution fusion | flops 34079232 | bytes 3145792 | tf_op jit(solution)/shard_map/dot_general | solution.py:75
  128.1 31.3 %all-to-all-done = bf16[16,512,128]{2,1,0:T(8,128)(2,1)} async-done(((bf16[16,512,128]{2,1,0:T(8,128)(2,1)}), bf16[16,512,128]{2,1,0:T(8,128)(2,1)}, u32[]{:S(2)}, u32[]{:S(2)}) %all-to-all-start) | async-done | bytes 2097184 | tf_op jit(solution)/shard_map/all_to_all | solution.py:27
  159.4 2.4 stack.2
  161.8 4.6 %all-to-all-start.3 = ((bf16[16,512,128]{1,2,0:T(8,128)(2,1)}), bf16[16,512,128]{1,2,0:T(8,128)(2,1)}, u32[]{:S(2)}, u32[]{:S(2)}) async-start(bf16[16,512,128]{1,2,0:T(8,128)(2,1)} %stack.2), calls=%async_computation.3 | async-start | bytes 4194304 | tf_op jit(solution)/shard_map/all_to_all | solution.py:12
  166.5 12.8 %all-gather.2.cloned.1.call-done = bf16[16,16,32,128]{3,2,1,0:T(8,128)(2,1)} async-done(((bf16[1,16,32,128]{3,2,1,0:T(8,128)(2,1)}), bf16[16,16,32,128]{3,2,1,0:T(8,128)(2,1)}) %all-gather.2.cloned.1.call-update) | async-done | bytes 2097168 | tf_op jit(solution)/shard_map/all_gather | solution.py:17
  179.3 1.9 reduce
  183.6 2.7 reduce.4
  186.3 2.2 reshape.125
  188.5 27.9 %all-to-all-done.3 = bf16[16,512,128]{1,2,0:T(8,128)(2,1)} async-done(((bf16[16,512,128]{1,2,0:T(8,128)(2,1)}), bf16[16,512,128]{1,2,0:T(8,128)(2,1)}, u32[]{:S(2)}, u32[]{:S(2)}) %all-to-all-start.3) | async-done | bytes 2097184 | tf_op jit(solution)/shard_map/all_to_all | solution.py:12
  216.4 5.2 %all-to-all-start.5 = ((bf16[32,2,4096]{2,1,0:T(2,128)(2,1)}), bf16[32,2,4096]{2,1,0:T(2,128)(2,1)}, u32[]{:S(2)}, u32[]{:S(2)}) async-start(bf16[32,2,4096]{2,1,0:T(2,128)(2,1)} %reshape.125), calls=%async_computation.5 | async-start | bytes 1048576 | tf_op jit(solution)/shard_map/all_to_all | solution.py:129
  224.0 2.1 fusion.1
  226.1 4.6 %reduce.3 = bf16[32,32768]{1,0:T(8,128)(2,1)} reduce(bf16[32,1,32768]{2,0,1:T(8,128)(2,1)} %fusion.1, bf16[]{:T(256)} %broadcast.31), dimensions={1}, to_apply=%copy.29.reduce_sub_computation | reduce | bytes 4194306 | tf_op jit(solution)/shard_map/all_to_all | solution.py:128
  230.7 4.5 %reshape.123 = bf16[32,2,16384]{2,1,0:T(2,128)(2,1)} reshape(bf16[32,32768]{1,0:T(8,128)(2,1)} %reduce.3) | data formatting | bytes 4194304
  235.2 3.3 %all-to-all-done.5 = bf16[32,2,4096]{2,1,0:T(2,128)(2,1)} async-done(((bf16[32,2,4096]{2,1,0:T(2,128)(2,1)}), bf16[32,2,4096]{2,1,0:T(2,128)(2,1)}, u32[]{:S(2)}, u32[]{:S(2)}) %all-to-all-start.5) | async-done | bytes 524320 | tf_op jit(solution)/shard_map/all_to_all | solution.py:129
  238.5 6.5 %all-to-all-start.4 = ((bf16[32,2,16384]{2,1,0:T(2,128)(2,1)}), bf16[32,2,16384]{2,1,0:T(2,128)(2,1)}, u32[]{:S(2)}, u32[]{:S(2)}) async-start(bf16[32,2,16384]{2,1,0:T(2,128)(2,1)} %reshape.123), calls=%async_computation.4 | async-start | bytes 4194304 | tf_op jit(solution)/shard_map/all_to_all | solution.py:128
  245.1 1.9 convert_reduce_fusion
  248.2 3.7 %fusion.9 = bf16[512,512]{1,0:T(8,128)(2,1)} fusion(f32[512,512]{1,0:T(8,128)S(1)} %bitcast.104, bf16[512,2048]{0,1:T(8,128)(2,1)} %bitcast.11, bf16[512,2048]{1,0:T(8,128)(2,1)S(1)} %copy-done), kind=kOutput, calls=%fused_computation.23 | convolution fusion | flops 1074266112 | bytes 5767168 | tf_op jit(solution)/shard_map/dot_general | solution.py:98
  251.9 3.6 %reshape.126 = bf16[32,1,8192]{2,1,0:T(2,128)(2,1)S(1)} reshape(bf16[32,2,4096]{2,1,0:T(2,128)(2,1)} %all-to-all-done.5) | data formatting | bytes 1048576
  256.9 37.6 %all-to-all-done.4 = bf16[32,2,16384]{2,1,0:T(2,128)(2,1)} async-done(((bf16[32,2,16384]{2,1,0:T(2,128)(2,1)}), bf16[32,2,16384]{2,1,0:T(2,128)(2,1)}, u32[]{:S(2)}, u32[]{:S(2)}) %all-to-all-start.4) | async-done | bytes 2097184 | tf_op jit(solution)/shard_map/all_to_all | solution.py:128
  294.4 10.5 %reshape.124 = bf16[32,1,32768]{2,1,0:T(2,128)(2,1)} reshape(bf16[32,2,16384]{2,1,0:T(2,128)(2,1)} %all-to-all-done.4) | data formatting | bytes 4194304
  304.9 4.5 %convolution_multiply_fusion = f32[3,32768]{1,0:T(4,128)S(1)} fusion(bf16[32,3]{0,1:T(4,128)(2,1)S(1)} %get-tuple-element.5, bf16[32,1,32768]{2,1,0:T(2,128)(2,1)} %reshape.124, f32[3]{0:T(128)S(1)} %maximum_divide_fusion), kind=kOutput, calls=%fused_computation.5 | convolution fusion | flops 6389760 | bytes 2490572 | tf_op jit(solution)/shard_map/dot_general | solution.py:133
  (46 shorter events, 19.1 us)
Async XLA Ops:
  7.2 41.1 %copy-start = (bf16[512,2048]{1,0:T(8,128)(2,1)S(1)}, bf16[512,2048]{1,0:T(8,128)(2,1)}, u32[]{:S(2)}) copy-start(bf16[512,2048]{1,0:T(8,128)(2,1)} %param.8) | copy-start | bytes 6291460
  7.2 18.6 %copy-start.6 = (bf16[3,64,512]{2,1,0:T(8,128)(2,1)S(1)}, bf16[3,64,512]{2,1,0:T(8,128)(2,1)}, u32[]{:S(2)}) copy-start(bf16[3,64,512]{2,1,0:T(8,128)(2,1)} %param.9) | copy-start | bytes 589828
  12.4 30.3 %all-to-all-start.2 = ((bf16[32,2,4096]{2,1,0:T(2,128)(2,1)}), bf16[32,2,4096]{2,1,0:T(2,128)(2,1)S(1)}, u32[]{:S(2)}, u32[]{:S(2)}) async-start(bf16[32,2,4096]{2,1,0:T(2,128)(2,1)} %reshape.119), calls=%async_computation.2 | async-start | bytes 1048576 | tf_op jit(solution)/shard_map/all_to_all | solution.py:73
  37.1 11.2 %copy-start.2 = (bf16[512,512]{1,0:T(8,128)(2,1)S(1)}, bf16[512,512]{1,0:T(8,128)(2,1)}, u32[]{:S(2)}) copy-start(bf16[512,512]{1,0:T(8,128)(2,1)} %param.7) | copy-start | bytes 1572868
  42.6 6.9 %copy-start.1 = (bf16[32,2,4096]{2,1,0:T(2,128)(2,1)}, bf16[32,2,4096]{2,1,0:T(2,128)(2,1)S(1)}, u32[]{:S(2)}) copy-start(bf16[32,2,4096]{2,1,0:T(2,128)(2,1)S(1)} %all-to-all-done.2) | copy-start | bytes 1572868
  42.6 55.3 %all-to-all-start.1 = ((bf16[32,2,16384]{2,1,0:T(2,128)(2,1)}), bf16[32,2,16384]{2,1,0:T(2,128)(2,1)}, u32[]{:S(2)}, u32[]{:S(2)}) async-start(bf16[32,2,16384]{2,1,0:T(2,128)(2,1)} %reshape.121), calls=%async_computation.1 | async-start | bytes 4194304 | tf_op jit(solution)/shard_map/all_to_all | solution.py:72
  98.0 61.5 %all-to-all-start = ((bf16[16,512,128]{2,1,0:T(8,128)(2,1)}), bf16[16,512,128]{2,1,0:T(8,128)(2,1)}, u32[]{:S(2)}, u32[]{:S(2)}) async-start(bf16[16,512,128]{2,1,0:T(8,128)(2,1)} %bitcast.92), calls=%async_computation | async-start | bytes 4194304 | tf_op jit(solution)/shard_map/all_to_all | solution.py:27
  105.2 4.5 %copy-start.4 = (bf16[512,128]{1,0:T(8,128)(2,1)S(1)}, bf16[512,128]{1,0:T(8,128)(2,1)}, u32[]{:S(2)}) copy-start(bf16[512,128]{1,0:T(8,128)(2,1)} %param.11) | copy-start | bytes 393220
  105.2 74.1 %all-gather.2.cloned.1.call-start = ((), (), s32[]{:S(2)}) async-start(), calls=%async_computation.6 | async-start | bytes 2228224 | tf_op jit(solution)/shard_map/all_gather | solution.py:17
  121.1 4.9 %copy-start.3 = (bf16[512,512]{1,0:T(8,128)(2,1)S(1)}, bf16[512,512]{1,0:T(8,128)(2,1)}, u32[]{:S(2)}) copy-start(bf16[512,512]{1,0:T(8,128)(2,1)} %param.7) | copy-start | bytes 1572868
  125.7 0.9 copy-start.5
  161.8 54.6 %all-to-all-start.3 = ((bf16[16,512,128]{1,2,0:T(8,128)(2,1)}), bf16[16,512,128]{1,2,0:T(8,128)(2,1)}, u32[]{:S(2)}, u32[]{:S(2)}) async-start(bf16[16,512,128]{1,2,0:T(8,128)(2,1)} %stack.2), calls=%async_computation.3 | async-start | bytes 4194304 | tf_op jit(solution)/shard_map/all_to_all | solution.py:12
  216.4 22.1 %all-to-all-start.5 = ((bf16[32,2,4096]{2,1,0:T(2,128)(2,1)}), bf16[32,2,4096]{2,1,0:T(2,128)(2,1)}, u32[]{:S(2)}, u32[]{:S(2)}) async-start(bf16[32,2,4096]{2,1,0:T(2,128)(2,1)} %reshape.125), calls=%async_computation.5 | async-start | bytes 1048576 | tf_op jit(solution)/shard_map/all_to_all | solution.py:129
  238.5 55.9 %all-to-all-start.4 = ((bf16[32,2,16384]{2,1,0:T(2,128)(2,1)}), bf16[32,2,16384]{2,1,0:T(2,128)(2,1)}, u32[]{:S(2)}, u32[]{:S(2)}) async-start(bf16[32,2,16384]{2,1,0:T(2,128)(2,1)} %reshape.123), calls=%async_computation.4 | async-start | bytes 4194304 | tf_op jit(solution)/shard_map/all_to_all | solution.py:128
Sparse Core Ops, SparseCore 0:
  127.5 51.7 all-gather.1
